TPU v7x, 512 devices: a whole 4x4x16 slice. The times are simulated.
512 devices in a mesh: dp: 64 (over z, y), tensor: 8 (over x, core).
Axes of the slice: x: 4, y: 4, z: 16, core: 2. Of those that a mesh axis runs over, the one named last changes fastest.
Arguments:
- queries: bfloat16 [32768, 8192], P('dp', 'tensor'), may hold values from -8 to 8
- key_heads: bfloat16 [32768, 1024], P('dp', 'tensor'), may hold values from -8 to 8
- value_heads: bfloat16 [32768, 1024], P('dp', 'tensor'), may hold values from -200 to 200
- doc_lengths: int32 [256], replicated, may hold values from 1 to 512, 32768 in all
Outputs:
- hessian: float32 [8, 1024, 1024], P('tensor', 'dp')
Inputs may be any that keep to these rules, and one draw needn't show every extreme that they name: `doc_lengths`: every document fits in 512 tokens; one document has exactly 512.
All inputs are finite; a program needn't handle non-finite values.
Results may differ from a plain program's by a relative error of at most 0.0006.
Values may be sent and summed in bfloat16 or wider, within the bound.
A program may use at most 128 MiB of HBM per device.

v0:
```python
import math

import jax
import jax.numpy as jnp
from jax import lax
from jax.sharding import PartitionSpec as P

HEADS = 64
HD = 128


damping = 0.01


def passed_along(value, axis, steps):
    count = lax.axis_size(axis)
    first, last = (max(0, -steps), min(count, count - steps))
    return lax.ppermute(value, axis, [(source, source + steps) for source in range(first, last)])


def on_device(queries, key_heads, value_heads, doc_lengths):
    tok_rows = queries.shape[0]
    groups = key_heads.shape[1] // HD
    per_group = queries.shape[1] // HD // groups
    group_width = per_group * HD
    inv_root = 1.0 / math.sqrt(HD)
    shard_index = lax.axis_index("dp")
    prev_keys, prev_values = passed_along((key_heads, value_heads), "dp", 1)
    all_keys = jnp.concatenate([prev_keys, key_heads], axis=0).reshape(2 * tok_rows, groups, HD)
    all_values = jnp.concatenate([prev_values, value_heads], axis=0).reshape(
        2 * tok_rows, groups, HD
    )
    starts = jnp.cumsum(doc_lengths, dtype=jnp.int32) - doc_lengths
    first_row = shard_index * tok_rows
    query_pos = first_row + jnp.arange(tok_rows, dtype=jnp.int32)
    key_pos = first_row - tok_rows + jnp.arange(2 * tok_rows, dtype=jnp.int32)
    doc_start = jnp.max(
        jnp.where(starts[None, :] <= query_pos[:, None], starts[None, :], 0), axis=1
    )
    visible = (key_pos[None, :] >= doc_start[:, None]) & (key_pos[None, :] <= query_pos[:, None])
    grouped_q = queries.reshape(tok_rows, groups, per_group, HD)

    def one_head(head_index):
        head_q = lax.dynamic_index_in_dim(grouped_q, head_index, 2, keepdims=False)
        scores = (
            jnp.einsum("tgd,sgd->gts", head_q, all_keys, preferred_element_type=jnp.float32)
            * inv_root
        )
        scores = jnp.where(visible[None], scores, -1e30)
        row_peak = jnp.max(scores, axis=-1)
        exponent = jnp.exp(scores - row_peak[..., None])
        row_total = jnp.sum(exponent, axis=-1)
        weights = exponent.astype(jnp.bfloat16)
        blended = jnp.einsum(
            "gts,sgd->tgd", weights, all_values, preferred_element_type=jnp.float32
        )
        return (blended / row_total.T[..., None]).astype(jnp.bfloat16)

    head_outs = lax.map(one_head, jnp.arange(per_group, dtype=jnp.int32))
    attended = jnp.transpose(head_outs, (1, 2, 0, 3)).reshape(tok_rows, groups, group_width)
    shard_count = lax.axis_size("dp")
    own_rows = group_width // shard_count
    gram_term = jnp.einsum("tgr,tgc->grc", attended, attended, preferred_element_type=jnp.float32)
    hess_rows = lax.psum_scatter(gram_term, "dp", scatter_dimension=1, tiled=True)
    row_ids = shard_index * own_rows + jnp.arange(own_rows, dtype=jnp.int32)
    diag_mask = row_ids[:, None] == jnp.arange(group_width, dtype=jnp.int32)[None, :]
    own_diag = jnp.sum(jnp.where(diag_mask[None], hess_rows, 0.0))
    energy = lax.psum(own_diag, ("dp", "tensor"))
    return hess_rows * (HEADS * HD / energy) + damping * diag_mask.astype(jnp.float32)[None]


def solution(mesh):
    placed = (P("dp", "tensor"), P("dp", "tensor"), P("dp", "tensor"), P())
    return jax.shard_map(
        on_device, mesh=mesh, in_specs=placed, out_specs=P("tensor", "dp", None), check_vma=False
    )
```

profile of v0, /device:TPU:24, one launch (start us, length us, event | category | flops | bytes accessed | tf_op | source)
XLA Modules:
  0.0 873.3 jit_solution(7034548446926816242)
XLA Ops:
  6.5 3.6 collective-permute-start
  10.2 3.5 collective-permute-start.1
  13.6 1.0 reduce-window.9
  14.9 0.8 bitcast_subtract_fusion
  15.9 1.5 copy.9
  17.5 37.7 %while.11 = (s32[]{:T(128)}, bf16[8,512,1,128]{1,3,0,2:T(8,128)(2,1)S(1)}, s32[8]{0:T(128)S(1)}, bf16[512,1,8,128]{0,3,2,1:T(8,128)(2,1)S(1)}, bf16[1024,1,128]{...) while((s32[]{:T(128)}, ...), condition=%wide.region_6.7_spmd.clone, body=%wide.region_3.6_spmd.clone.sunk | while | flops 273808384 | bytes 7620787 | solution.py:59
  17.5 0.7 dynamic_slice.19
  20.2 0.8 fusion.24
  21.0 0.5 fusion.25
  22.2 0.7 dynamic_slice.19
  25.0 0.8 fusion.24
  25.7 0.5 fusion.25
  26.9 0.7 dynamic_slice.19
  29.7 0.8 fusion.24
  30.4 0.5 fusion.25
  31.6 0.7 dynamic_slice.19
  34.4 0.8 fusion.24
  35.2 0.5 fusion.25
  36.3 0.7 dynamic_slice.19
  39.1 0.8 fusion.24
  41.1 0.7 dynamic_slice.19
  43.8 0.8 fusion.24
  45.8 0.7 dynamic_slice.19
  48.5 0.8 fusion.24
  50.5 0.7 dynamic_slice.19
  53.2 0.8 fusion.24
  54.0 0.5 fusion.25
  55.2 3.2 convolution_bitcast_fusion.1
  58.4 703.6 %reduce-scatter.2.cloned.1.call-done = f32[1,16,1024]{2,1,0:T(8,128)} async-done(((f32[1,1024,1024]{2,1,0:T(8,128)}), f32[1,16,1024]{2,1,0:T(8,128)}) %reduce-scatter.2.cloned.1.call-update) | async-done | bytes 65552 | tf_op jit(solution)/shard_map/reduce_scatter | solution.py:64
  762.0 1.5 select_reduce_fusion.1
  763.5 100.7 %psum.7 = f32[]{:T(128)} all-reduce(f32[]{:T(128)} %select_reduce_fusion.1), channel_id=1, replica_groups=mesh['dp'=64,'tensor'=8] {'dp','tensor'}, use_global_device_ids=true, to_apply=%region_9.10 | all-reduce | flops 1 | bytes 8 | tf_op jit(solution)/shard_map/psum | solution.py:68
  864.9 1.5 select_add_fusion
  (46 shorter events, 7.2 us)
Async XLA Ops:
  6.5 10.9 %copy-start = (bf16[512,128]{1,0:T(8,128)(2,1)S(1)}, bf16[512,128]{1,0:T(8,128)(2,1)}, u32[]{:S(2)}) copy-start(bf16[512,128]{1,0:T(8,128)(2,1)} %param.7) | copy-start | bytes 393220
  6.5 10.9 %copy-start.1 = (bf16[512,128]{1,0:T(8,128)(2,1)S(1)}, bf16[512,128]{1,0:T(8,128)(2,1)}, u32[]{:S(2)}) copy-start(bf16[512,128]{1,0:T(8,128)(2,1)} %param.8) | copy-start | bytes 393220
  6.5 755.5 %reduce-scatter.2.cloned.1.call-start = ((), (), s32[]{:S(2)}) async-start(), calls=%async_computation.1 | async-start | bytes 4259840 | tf_op jit(solution)/shard_map/reduce_scatter | solution.py:64
  6.5 10.8 %collective-permute-start = (bf16[512,128]{1,0:T(8,128)(2,1)}, bf16[512,128]{1,0:T(8,128)(2,1)S(1)}, u32[]{:S(2)}, u32[]{:S(2)}) collective-permute-start(bf16[512,128]{1,0:T(8,128)(2,1)} %param.7), channel_id=1, source_target_pairs={{0,8},{8,16},{16,24},{24,32},{32,40},{40,48},{48,56},{56,64},{64,7... | collective-permute-start | bytes 393224 | tf_op jit(solution)/shard_map/ppermute | solution.py:18
  10.2 7.3 collective-permute-start.1
Sparse Core Ops, SparseCore 0:
  58.5 703.4 reduce-scatter.1
where the time goes:
time: 877 us; the launch traced here: 873 us
  waiting for transfers between devices  704 us (80%)
  blocking collectives  101 us (12%)
  loops' own time  16.9 us (2%)
  between operations  14.2 us (2%)
  matrix products  13.5 us (2%)
  other arithmetic  9.26 us (1%)
    reduce_scatter x1, waiting for transfers between devices, on_device(): lax.psum_scatter(gram_term, 'dp', scatter_dimension=1, tiled=True)  704 us
    psum x1, blocking collectives, on_device(): energy = lax.psum(own_diag, ('dp', 'tensor'))  101 us
  transfers between devices with their start and end apart: 3, of which 1 were waited for; matrix products, arithmetic and copies ran while one was open for 0% of the time, Pallas kernels for 0%

commit v1 on v0

v1 whole, which is shorter than its diff:
```python
import functools
import math

import jax
import jax.numpy as jnp
from jax import lax
from jax.experimental import pallas as pl
from jax.experimental.pallas import tpu as pltpu
from jax.sharding import PartitionSpec as P

HEADS = 64
HD = 128
TOK = 512
QB = 128
WIN = TOK + QB
NZ, NY, NT = 16, 4, 8
PAIRS = 4
FULL = 32767.0
MESH = pl.DeviceIdType.MESH
F32 = jnp.float32

damping = 0.01


def passed_along(value, axis, steps):
    count = lax.axis_size(axis)
    first, last = (max(0, -steps), min(count, count - steps))
    return lax.ppermute(value, axis, [(source, source + steps) for source in range(first, last)])


def z_of(pair, quarter):
    return 2 * pair + quarter % 2 + 8 * (quarter // 2)


def piece_blocks(stage, part):
    if part == 0:
        return stage * stage, [(stage, col) for col in range(stage + 1)]
    return stage * stage + stage + 1, [(row, stage) for row in range(stage)]


PIECES = [(s, p) for s in range(PAIRS) for p in range(2) if p == 0 or s > 0]


def to_fixed(block):
    peak = jnp.maximum(jnp.max(jnp.abs(block), axis=0, keepdims=True), 1e-30)
    fixed = jnp.round(block * (FULL / peak)).astype(jnp.int32).astype(jnp.int16)
    return fixed, peak * (1.0 / FULL)


def from_fixed(fixed, scale):
    return fixed.astype(jnp.int32).astype(F32) * scale


def kernel(
    len_ref, q_ref, kp_ref, ko_ref, vp_ref, vo_ref, out_ref,
    keys, vt, bias, at, gs, own, yq, yqs, yr, yrs, zq, zqs, zr, zrs, en, ent, eny, enz,
    y_send, y_recv, z_send, z_recv, e_send, e_recv,
):
    dp = lax.axis_index("dp")
    t = lax.axis_index("tensor")
    z, y = lax.div(dp, NY), lax.rem(dp, NY)
    first_row = dp * TOK

    def z_peer(d):
        return (lax.rem(z + d, NZ) * NY + y, t)

    def y_peer(d):
        return (z * NY + lax.rem(y + d, NY), t)

    def t_peer(d):
        return (dp, lax.rem(t + d, NT))

    barrier = pltpu.get_barrier_semaphore()
    peers = [y_peer(d) for d in range(1, NY)] + [t_peer(d) for d in range(1, NT)]
    peers += [z_peer(d) for d in range(1, NZ)]
    for peer in peers:
        pl.semaphore_signal(barrier, inc=1, device_id=peer, device_id_type=MESH)

    def remote(src, dst, send, recv, peer):
        return pltpu.make_async_remote_copy(
            src_ref=src, dst_ref=dst, send_sem=send, recv_sem=recv, device_id=peer, device_id_type=MESH
        )

    def wait_for(ref, sem):
        pltpu.make_async_copy(ref, ref, sem).wait()

    keys[0:TOK] = kp_ref[...]
    keys[TOK:] = ko_ref[...]
    vt[:, 0:TOK] = vp_ref[...].T
    vt[:, TOK:] = vo_ref[...].T

    lens = len_ref[...].astype(F32)
    n_docs = lens.shape[1]
    before = lax.broadcasted_iota(jnp.int32, (n_docs, n_docs), 1) < lax.broadcasted_iota(
        jnp.int32, (n_docs, n_docs), 0
    )
    starts = jnp.sum(jnp.where(before, lens, 0.0), axis=1, keepdims=True)
    position = (first_row + lax.broadcasted_iota(jnp.int32, (1, TOK), 1)).astype(F32)
    doc_start = jnp.max(jnp.where(starts <= position, starts, 0.0), axis=0, keepdims=True)
    for b in range(TOK // QB):
        key_pos = (first_row - TOK + b * QB + lax.broadcasted_iota(jnp.int32, (WIN, QB), 0)).astype(F32)
        cols = slice(b * QB, (b + 1) * QB)
        visible = (key_pos >= doc_start[:, cols]) & (key_pos <= position[:, cols])
        bias[b] = jnp.where(visible, 0.0, -1e30)

    factor = math.log2(math.e) / math.sqrt(HD)

    def attend(pair, b, energy):
        rows = pl.ds(pl.multiple_of(b * QB, QB), QB)
        window = pl.ds(pl.multiple_of(b * QB, QB), WIN)
        two = jnp.concatenate(
            [q_ref[rows, h * HD : (h + 1) * HD] for h in (pair, pair + PAIRS)], axis=0
        )
        scores = lax.dot_general(
            keys[window, :], two, (((1,), (1,)), ((), ())), preferred_element_type=F32
        )
        mask = bias[b]
        scores = scores * factor + jnp.concatenate([mask, mask], axis=1)
        peak = jnp.max(scores, axis=0, keepdims=True)
        exponent = jnp.exp2(scores - peak)
        total = jnp.sum(exponent, axis=0, keepdims=True)
        blended = lax.dot_general(
            vt[:, window], exponent.astype(jnp.bfloat16), (((1,), (0,)), ((), ())), preferred_element_type=F32
        )
        attended = (blended * (1.0 / total)).astype(jnp.bfloat16)
        at[pair, 0:HD, rows] = attended[:, 0:QB]
        at[pair, HD:, rows] = attended[:, QB:]
        wide = attended.astype(F32)
        return energy + jnp.sum(wide * wide, axis=0, keepdims=True)

    def gram_block(k, row, col):
        block = lax.dot_general(at[row], at[col], (((1,), (1,)), ((), ())), preferred_element_type=F32)
        gs[...] = block
        fixed, scale = to_fixed(block)
        yqs[k] = scale
        for q in range(4):
            for a in range(NY):
                low = q * 64 + a * 16
                yq[a, k, q * 16 : (q + 1) * 16, :] = fixed[low : low + 16, :]
            own[k, q * 16 : (q + 1) * 16, :] = gs[pl.ds(pl.multiple_of(q * 64 + y * 16, 16), 16), :]

    def y_stage(piece):
        first, blocks = piece_blocks(*PIECES[piece])
        for i, (row, col) in enumerate(blocks):
            gram_block(first + i, row, col)
        span = pl.ds(first, len(blocks))
        for d in range(1, NY):
            peer = y_peer(d)
            to = lax.rem(y + d, NY)
            remote(yqs.at[span], yrs.at[d - 1, span], y_send.at[1, piece], y_recv.at[1, piece], peer).start()
            remote(yq.at[to, span], yr.at[d - 1, span], y_send.at[0, piece], y_recv.at[0, piece], peer).start()

    sent = []

    def z_stage(piece):
        stage, part = PIECES[piece]
        first, blocks = piece_blocks(stage, part)
        span = pl.ds(first, len(blocks))
        wait_for(yrs.at[:, span], y_recv.at[1, piece])
        wait_for(yr.at[:, span], y_recv.at[0, piece])
        for k in range(first, first + len(blocks)):
            total = own[k]
            for d in range(NY - 1):
                total = total + from_fixed(yr[d, k], yrs[d, k])
            own[k] = total
            fixed, scale = to_fixed(total)
            zqs[k] = scale
            for q in range(4):
                zq[k, q] = fixed[q * 16 : (q + 1) * 16, :]
        if part == 0:
            targets = [(stage, first, len(blocks), 0)]
        else:
            targets = [(row, first + row, 1, stage) for row in range(stage)]
        for row, k, count, slot in targets:
            for q in range(4):
                target = z_of(row, q)
                n = len(sent)
                place = lax.rem(z - target + NZ, NZ) - 1

                def copies(target=target, n=n, place=place, q=q, k=k, count=count, slot=slot):
                    kinds = (
                        (zq.at[pl.ds(k, count), q], zr.at[place, pl.ds(slot, count)]),
                        (zqs.at[pl.ds(k, count)], zrs.at[place, pl.ds(slot, count)]),
                    )
                    sem = slot if part == 1 else 0
                    return [
                        remote(src, dst, z_send.at[i, n], z_recv.at[i, sem], (target * NY + y, t))
                        for i, (src, dst) in enumerate(kinds)
                    ]

                sent.append((target, copies))

                @pl.when(z != target)
                def _(copies=copies):
                    for copy in copies():
                        copy.start()

    energy = jnp.zeros((1, 2 * QB), F32)
    for pair in range(PAIRS):
        energy = lax.fori_loop(0, TOK // QB, functools.partial(attend, pair), energy)
        if pair == 0:
            pl.semaphore_wait(barrier, len(peers))
        if pair == PAIRS - 1:
            en[0] = energy[:, 0:QB] + energy[:, QB:]
            for d in range(1, NT):
                remote(en.at[0], ent.at[d - 1], e_send.at[0], e_recv.at[0], t_peer(d)).start()
        for piece, (stage, part) in enumerate(PIECES):
            if stage == pair - 2:
                z_stage(piece)
        for piece, (stage, part) in enumerate(PIECES):
            if stage == pair:
                y_stage(piece)
    wait_for(ent, e_recv.at[0])
    en[1] = en[0] + jnp.sum(ent[...], axis=0)
    for d in range(1, NY):
        remote(en.at[1], eny.at[d - 1], e_send.at[1], e_recv.at[1], y_peer(d)).start()
    for piece, (stage, part) in enumerate(PIECES):
        if stage == PAIRS - 2:
            z_stage(piece)
    wait_for(eny, e_recv.at[1])
    en[2] = en[1] + jnp.sum(eny[...], axis=0)
    for d in range(1, NZ):
        remote(en.at[2], enz.at[d - 1], e_send.at[2], e_recv.at[2], z_peer(d)).start()
    for piece, (stage, part) in enumerate(PIECES):
        if stage == PAIRS - 1:
            z_stage(piece)

    my_pair = lax.div(lax.rem(z, 8), 2)
    my_quarter = 2 * lax.div(z, 8) + lax.rem(z, 2)
    wait_for(enz, e_recv.at[2])
    all_energy = jnp.sum(en[2] + jnp.sum(enz[...], axis=0), axis=1, keepdims=True)
    gain = (HEADS * HD) / all_energy
    for s in range(PAIRS):

        @pl.when(my_pair == s)
        def _(s=s):
            wait_for(zrs.at[:, pl.ds(0, s + 1)], z_recv.at[1, 0])
            wait_for(zr.at[:, pl.ds(0, s + 1)], z_recv.at[0, 0])

    for s in range(1, PAIRS):

        @pl.when(my_pair < s)
        def _(s=s):
            wait_for(zrs.at[:, s], z_recv.at[1, s])
            wait_for(zr.at[:, s], z_recv.at[0, s])

    row_id = dp * 16 + lax.broadcasted_iota(jnp.int32, (16, HD), 0)
    col_id = lax.broadcasted_iota(jnp.int32, (16, HD), 1)
    my_rows = pl.ds(pl.multiple_of(my_quarter * 16, 16), 16)
    for col in range(PAIRS):
        k = jnp.where(my_pair >= col, my_pair * my_pair + col, col * col + col + 1 + my_pair)
        total = own[k, my_rows, :]
        for d in range(NZ - 1):
            total = total + from_fixed(zr[d, col], zrs[d, col])
        for half in range(2):
            head = col + PAIRS * half
            part = total[:, half * HD : (half + 1) * HD] * gain
            eye = jnp.where(row_id == col_id + head * HD, damping, 0.0)
            out_ref[:, head * HD : (head + 1) * HD] = part + eye

    for piece, (stage, part) in enumerate(PIECES):
        first, blocks = piece_blocks(stage, part)
        span = pl.ds(first, len(blocks))
        wait_for(yrs.at[:, span], y_send.at[1, piece])
        wait_for(yr.at[:, span], y_send.at[0, piece])
    for target, copies in sent:

        @pl.when(z != target)
        def _(copies=copies):
            for copy in copies():
                copy.wait_send()

    wait_for(ent, e_send.at[0])
    wait_for(eny, e_send.at[1])
    wait_for(enz, e_send.at[2])


def on_device(queries, key_heads, value_heads, doc_lengths):
    prev_keys, prev_values = passed_along((key_heads, value_heads), "dp", 1)
    blocks = PAIRS * PAIRS
    width = 2 * HD
    n_sent = sum(len(piece_blocks(s, 1)[1]) + 1 for s in range(PAIRS)) * 4
    vmem = pl.BlockSpec(memory_space=pltpu.VMEM)
    rows = pl.pallas_call(
        kernel,
        out_shape=jax.ShapeDtypeStruct((16, 8 * HD), F32),
        in_specs=[vmem] * 6,
        out_specs=vmem,
        scratch_shapes=[
            pltpu.VMEM((2 * TOK, HD), jnp.bfloat16),
            pltpu.VMEM((HD, 2 * TOK), jnp.bfloat16),
            pltpu.VMEM((TOK // QB, WIN, QB), F32),
            pltpu.VMEM((PAIRS, width, TOK), jnp.bfloat16),
            pltpu.VMEM((width, width), F32),
            pltpu.VMEM((blocks, 64, width), F32),
            pltpu.VMEM((NY, blocks, 64, width), jnp.int16),
            pltpu.VMEM((blocks, 1, width), F32),
            pltpu.VMEM((NY - 1, blocks, 64, width), jnp.int16),
            pltpu.VMEM((NY - 1, blocks, 1, width), F32),
            pltpu.VMEM((blocks, 4, 16, width), jnp.int16),
            pltpu.VMEM((blocks, 1, width), F32),
            pltpu.VMEM((NZ - 1, PAIRS, 16, width), jnp.int16),
            pltpu.VMEM((NZ - 1, PAIRS, 1, width), F32),
            pltpu.VMEM((3, 1, HD), F32),
            pltpu.VMEM((NT - 1, 1, HD), F32),
            pltpu.VMEM((NY - 1, 1, HD), F32),
            pltpu.VMEM((NZ - 1, 1, HD), F32),
            pltpu.SemaphoreType.DMA((2, len(PIECES))),
            pltpu.SemaphoreType.DMA((2, len(PIECES))),
            pltpu.SemaphoreType.DMA((2, n_sent)),
            pltpu.SemaphoreType.DMA((2, PAIRS)),
            pltpu.SemaphoreType.DMA((3,)),
            pltpu.SemaphoreType.DMA((3,)),
        ],
        compiler_params=pltpu.CompilerParams(
            collective_id=0, has_side_effects=True, vmem_limit_bytes=48 << 20
        ),
        name="attend_and_gram",
    )(doc_lengths.reshape(1, -1), queries, prev_keys, key_heads, prev_values, value_heads)
    return rows[None]


def solution(mesh):
    placed = (P("dp", "tensor"), P("dp", "tensor"), P("dp", "tensor"), P())
    return jax.shard_map(
        on_device, mesh=mesh, in_specs=placed, out_specs=P("tensor", "dp", None), check_vma=False
    )
```

time: 877 us -> 76.1 us (0.09)
  the two profiles are of different devices: /device:TPU:24 before, /device:TPU:32 now
where the time goes in v1:
time: 76.1 us; the launch traced here: 75.8 us
  Pallas kernels  59.4 us (78%)
  starting transfers between devices  7.09 us (9%)
  waiting for transfers between devices  5.69 us (7%)
  local copies, waits for them, and re-layouts  3.67 us (5%)
    pallas_call x1, Pallas kernels, on_device(): pl.pallas_call(kernel, out_shape=jax.ShapeDtypeStruct((16, 8 * HD), F32),...  59.4 us
    ppermute x2, starting transfers between devices, passed_along(): lax.ppermute(value, axis, [(source, source + steps) for source in range(f...  7.09 us
    ppermute x2, waiting for transfers between devices, passed_along(): lax.ppermute(value, axis, [(source, source + steps) for source in range(f...  5.69 us
    unnamed x9, local copies, waits for them, and re-layouts  3.67 us
  transfers between devices with their start and end apart: 2, of which 2 were waited for; matrix products, arithmetic and copies ran while one was open for 0% of the time, Pallas kernels for 0%

profile of v1, /device:TPU:32, one launch (start us, length us, event | category | flops | bytes accessed | tf_op | source)
XLA Modules:
  0.0 75.8 jit_solution(16838532018521175649)
XLA Ops:
  0.0 0.0 copy-start.3
  0.0 3.6 %collective-permute-start = (bf16[512,128]{1,0:T(8,128)(2,1)}, bf16[512,128]{1,0:T(8,128)(2,1)S(1)}, u32[]{:S(2)}, u32[]{:S(2)}) collective-permute-start(bf16[512,128]{1,0:T(8,128)(2,1)} %ko_ref.1), channel_id=1, source_target_pairs={{0,8},{8,16},{16,24},{24,32},{32,40},{40,48},{48,56},{56,64},{64,7... | collective-permute-start | bytes 393224 | tf_op jit(solution)/shard_map/ppermute | solution.py:28
  3.6 3.5 %collective-permute-start.1 = (bf16[512,128]{1,0:T(8,128)(2,1)}, bf16[512,128]{1,0:T(8,128)(2,1)S(1)}, u32[]{:S(2)}, u32[]{:S(2)}) collective-permute-start(bf16[512,128]{1,0:T(8,128)(2,1)} %vo_ref.1), channel_id=1, source_target_pairs={{0,8},{8,16},{16,24},{24,32},{32,40},{40,48},{48,56},{56,64},{64,7... | collective-permute-start | bytes 393224 | tf_op jit(solution)/shard_map/ppermute | solution.py:28
  7.1 2.5 %collective-permute-done.kp_ref = bf16[512,128]{1,0:T(8,128)(2,1)S(1)} collective-permute-done((bf16[512,128]{1,0:T(8,128)(2,1)}, bf16[512,128]{1,0:T(8,128)(2,1)S(1)}, u32[]{:S(2)}, u32[]{:S(2)}) %collective-permute-start) | collective-permute-done | bytes 131104 | tf_op jit(solution)/shard_map/ppermute | solution.py:28
  9.6 3.2 %collective-permute-done.1.vp_ref = bf16[512,128]{1,0:T(8,128)(2,1)S(1)} collective-permute-done((bf16[512,128]{1,0:T(8,128)(2,1)}, bf16[512,128]{1,0:T(8,128)(2,1)S(1)}, u32[]{:S(2)}, u32[]{:S(2)}) %collective-permute-start.1) | collective-permute-done | bytes 131104 | tf_op jit(solution)/shard_map/ppermute | solution.py:28
  12.8 0.0 copy-done.3
  12.8 0.0 copy-start
  12.8 1.2 %copy-done = bf16[512,1024]{1,0:T(8,128)(2,1)S(1)} copy-done((bf16[512,1024]{1,0:T(8,128)(2,1)S(1)}, bf16[512,1024]{1,0:T(8,128)(2,1)}, u32[]{:S(2)}) %copy-start) | copy-done | bytes 1048600
  14.0 0.0 copy-start.1
  14.0 0.9 %copy-done.1 = bf16[512,128]{1,0:T(8,128)(2,1)S(1)} copy-done((bf16[512,128]{1,0:T(8,128)(2,1)S(1)}, bf16[512,128]{1,0:T(8,128)(2,1)}, u32[]{:S(2)}) %copy-start.1) | copy-done | bytes 131096
  14.9 0.0 copy-start.2
  14.9 0.9 %copy-done.2 = bf16[512,128]{1,0:T(8,128)(2,1)S(1)} copy-done((bf16[512,128]{1,0:T(8,128)(2,1)S(1)}, bf16[512,128]{1,0:T(8,128)(2,1)}, u32[]{:S(2)}) %copy-start.2) | copy-done | bytes 131096
  15.8 59.4 %attend_and_gram.1 = f32[16,1024]{1,0:T(8,128)S(1)} custom-call(s32[1,256]{1,0:T(1,128)S(1)} %bitcast.3, bf16[512,1024]{1,0:T(8,128)(2,1)S(1)} %copy-done, bf16[512,128]{1,0:T(8,128)(2,1)S(1)} %collective-permute-done.kp_ref, bf16[512,128]{1,0:T(8,128)(2,1)S(1)} %copy-done.1, bf16[512,128]{1,0:T(8,128)(2,1)S(1)} %collective-permute-done.1.vp_ref, ...), custom_call_target="tpu_custom_call" | custom-call | tf_op jit(solution)/shard_map/attend_and_gram/pallas_call | solution.py:284
  75.2 0.6 copy.6
Async XLA Ops:
  0.0 12.8 %copy-start.3 = (s32[256]{0:T(256)S(1)}, s32[256]{0:T(256)}, u32[]{:S(2)}) copy-start(s32[256]{0:T(256)} %param.7) | copy-start | bytes 3076
  0.0 9.6 %collective-permute-start = (bf16[512,128]{1,0:T(8,128)(2,1)}, bf16[512,128]{1,0:T(8,128)(2,1)S(1)}, u32[]{:S(2)}, u32[]{:S(2)}) collective-permute-start(bf16[512,128]{1,0:T(8,128)(2,1)} %ko_ref.1), channel_id=1, source_target_pairs={{0,8},{8,16},{16,24},{24,32},{32,40},{40,48},{48,56},{56,64},{64,7... | collective-permute-start | bytes 393224 | tf_op jit(solution)/shard_map/ppermute | solution.py:28
  3.6 9.2 %collective-permute-start.1 = (bf16[512,128]{1,0:T(8,128)(2,1)}, bf16[512,128]{1,0:T(8,128)(2,1)S(1)}, u32[]{:S(2)}, u32[]{:S(2)}) collective-permute-start(bf16[512,128]{1,0:T(8,128)(2,1)} %vo_ref.1), channel_id=1, source_target_pairs={{0,8},{8,16},{16,24},{24,32},{32,40},{40,48},{48,56},{56,64},{64,7... | collective-permute-start | bytes 393224 | tf_op jit(solution)/shard_map/ppermute | solution.py:28
  12.8 1.2 %copy-start = (bf16[512,1024]{1,0:T(8,128)(2,1)S(1)}, bf16[512,1024]{1,0:T(8,128)(2,1)}, u32[]{:S(2)}) copy-start(bf16[512,1024]{1,0:T(8,128)(2,1)} %q_ref.1) | copy-start | bytes 3145732
  14.0 0.9 %copy-start.1 = (bf16[512,128]{1,0:T(8,128)(2,1)S(1)}, bf16[512,128]{1,0:T(8,128)(2,1)}, u32[]{:S(2)}) copy-start(bf16[512,128]{1,0:T(8,128)(2,1)} %ko_ref.1) | copy-start | bytes 393220
  14.9 0.9 %copy-start.2 = (bf16[512,128]{1,0:T(8,128)(2,1)S(1)}, bf16[512,128]{1,0:T(8,128)(2,1)}, u32[]{:S(2)}) copy-start(bf16[512,128]{1,0:T(8,128)(2,1)} %vo_ref.1) | copy-start | bytes 393220

commit v2 on v1

v2 whole, which is shorter than its diff:
```python
import functools
import math

import jax
import jax.numpy as jnp
from jax import lax
from jax.experimental import pallas as pl
from jax.experimental.pallas import tpu as pltpu
from jax.sharding import PartitionSpec as P

HEADS = 64
HD = 128
TOK = 512
QB = 128
WIN = TOK + QB
NZ, NY, NT = 16, 4, 8
PAIRS = 4
FULL = 32767.0
MESH = pl.DeviceIdType.MESH
F32 = jnp.float32

damping = 0.01


RELAYS = (1, 5, 15, 11)
INPUTS = ((2, 3, 4), (6, 7, 8), (14, 13, 12), (10, 9))


def plan():
    pieces = []
    for stage in range(PAIRS):
        row = [(stage, col) for col in range(stage + 1)]
        if stage == PAIRS - 1:
            pieces.append((stage, row))
        else:
            pieces.append((stage, row))
        if stage > 0:
            pieces.append((stage, [(above, stage) for above in range(stage)]))
    return pieces


PIECES = plan()
FIRST = [sum(len(blocks) for _, blocks in PIECES[:n]) for n in range(len(PIECES))]
NUMBER = {block: k for k, block in enumerate(block for _, blocks in PIECES for block in blocks)}


def to_fixed(block):
    peak = jnp.maximum(jnp.max(jnp.abs(block), axis=0, keepdims=True), 1e-30)
    fixed = jnp.round(block * (FULL / peak)).astype(jnp.int32).astype(jnp.int16)
    return fixed, peak * (1.0 / FULL)


def from_fixed(fixed, scale):
    return fixed.astype(jnp.int32).astype(F32) * scale


def kernel(
    len_hbm, q_hbm, k_hbm, v_hbm, out_ref,
    lengths, q_ref, keys, vals, vt, bias, at, gs, own,
    yq, yqs, yr, yrs, zq, zqs, rr, rrs, rq, rqs, zr, zrs, en, ent, eny, enz,
    l_sem, h_send, h_recv, y_send, y_recv, r_send, r_recv, z_send, z_recv, e_send, e_recv,
):
    dp = lax.axis_index("dp")
    t = lax.axis_index("tensor")
    z, y = lax.div(dp, NY), lax.rem(dp, NY)
    first_row = dp * TOK

    def z_peer(d):
        return (lax.rem(z + d, NZ) * NY + y, t)

    def y_peer(d):
        return (z * NY + lax.rem(y + d, NY), t)

    def t_peer(d):
        return (dp, lax.rem(t + d, NT))

    following = (lax.rem(dp + 1, NZ * NY), t)
    preceding = (lax.rem(dp + NZ * NY - 1, NZ * NY), t)
    barrier = pltpu.get_barrier_semaphore()
    peers = [preceding] + [y_peer(d) for d in range(1, NY)] + [z_peer(d) for d in range(1, NZ)]
    peers += [t_peer(d) for d in range(1, NT)]
    for peer in peers:
        pl.semaphore_signal(barrier, inc=1, device_id=peer, device_id_type=MESH)

    def remote(src, dst, send, recv, peer):
        return pltpu.make_async_remote_copy(
            src_ref=src, dst_ref=dst, send_sem=send, recv_sem=recv, device_id=peer, device_id_type=MESH
        )

    def wait_for(ref, sem):
        pltpu.make_async_copy(ref, ref, sem).wait()

    earlier, later = pl.ds(0, TOK), pl.ds(TOK, TOK)
    loads = [(len_hbm, lengths), (k_hbm, keys.at[later]), (v_hbm, vals.at[later]), (q_hbm, q_ref)]
    loads = [pltpu.make_async_copy(src, dst, l_sem.at[n]) for n, (src, dst) in enumerate(loads)]
    for load in loads:
        load.start()

    pl.semaphore_wait(barrier, len(peers))
    halo = [
        remote(k_hbm, keys.at[earlier], h_send.at[0], h_recv.at[0], following),
        remote(v_hbm, vals.at[earlier], h_send.at[1], h_recv.at[1], following),
    ]
    for copy in halo:
        copy.start()

    loads[0].wait()
    lens = lengths[...].astype(F32)
    n_docs = lens.shape[1]
    before = lax.broadcasted_iota(jnp.int32, (n_docs, n_docs), 1) < lax.broadcasted_iota(
        jnp.int32, (n_docs, n_docs), 0
    )
    starts = jnp.sum(jnp.where(before, lens, 0.0), axis=1, keepdims=True)
    position = (first_row + lax.broadcasted_iota(jnp.int32, (1, TOK), 1)).astype(F32)
    doc_start = jnp.max(jnp.where(starts <= position, starts, 0.0), axis=0, keepdims=True)
    for b in range(TOK // QB):
        key_pos = (first_row - TOK + b * QB + lax.broadcasted_iota(jnp.int32, (WIN, QB), 0)).astype(F32)
        cols = slice(b * QB, (b + 1) * QB)
        visible = (key_pos >= doc_start[:, cols]) & (key_pos <= position[:, cols])
        bias[b] = jnp.where(visible, 0.0, -1e30)
    for load in loads[1:]:
        load.wait()
    vt[:, TOK:] = vals[TOK:].T
    for copy in halo:
        copy.wait_recv()
    vt[:, 0:TOK] = vals[0:TOK].T

    factor = math.log2(math.e) / math.sqrt(HD)

    def attend(pair, b, energy):
        rows = pl.ds(pl.multiple_of(b * QB, QB), QB)
        window = pl.ds(pl.multiple_of(b * QB, QB), WIN)
        two = jnp.concatenate(
            [q_ref[rows, h * HD : (h + 1) * HD] for h in (pair, pair + PAIRS)], axis=0
        )
        scores = lax.dot_general(
            keys[window, :], two, (((1,), (1,)), ((), ())), preferred_element_type=F32
        )
        mask = bias[b]
        scores = scores * factor + jnp.concatenate([mask, mask], axis=1)
        peak = jnp.max(scores, axis=0, keepdims=True)
        exponent = jnp.exp2(scores - peak)
        total = jnp.sum(exponent, axis=0, keepdims=True)
        blended = lax.dot_general(
            vt[:, window], exponent.astype(jnp.bfloat16), (((1,), (0,)), ((), ())), preferred_element_type=F32
        )
        attended = (blended * (1.0 / total)).astype(jnp.bfloat16)
        at[pair, 0:HD, rows] = attended[:, 0:QB]
        at[pair, HD:, rows] = attended[:, QB:]
        wide = attended.astype(F32)
        return energy + jnp.sum(wide * wide, axis=0, keepdims=True)

    def gram_block(k, row, col):
        block = lax.dot_general(at[row], at[col], (((1,), (1,)), ((), ())), preferred_element_type=F32)
        gs[...] = block
        fixed, scale = to_fixed(block)
        yqs[k] = scale
        for q in range(4):
            for a in range(NY):
                low = q * 64 + a * 16
                yq[a, k, q * 16 : (q + 1) * 16, :] = fixed[low : low + 16, :]
            own[k, q * 16 : (q + 1) * 16, :] = gs[pl.ds(pl.multiple_of(q * 64 + y * 16, 16), 16), :]

    def y_stage(piece):
        first, blocks = FIRST[piece], PIECES[piece][1]
        for i, (row, col) in enumerate(blocks):
            gram_block(first + i, row, col)
        span = pl.ds(first, len(blocks))
        for d in range(1, NY):
            peer = y_peer(d)
            to = lax.rem(y + d, NY)
            remote(yqs.at[span], yrs.at[d - 1, span], y_send.at[1, piece], y_recv.at[1, piece], peer).start()
            remote(yq.at[to, span], yr.at[d - 1, span], y_send.at[0, piece], y_recv.at[0, piece], peer).start()

    def z_stage(piece):
        first, blocks = FIRST[piece], PIECES[piece][1]
        span = pl.ds(first, len(blocks))
        wait_for(yrs.at[:, span], y_recv.at[1, piece])
        wait_for(yr.at[:, span], y_recv.at[0, piece])
        for k in range(first, first + len(blocks)):
            total = own[k]
            for d in range(NY - 1):
                total = total + from_fixed(yr[d, k], yrs[d, k])
            own[k] = total
            fixed, scale = to_fixed(total)
            zqs[k] = scale
            for q in range(4):
                zq[k, q] = fixed[q * 16 : (q + 1) * 16, :]
        for role, offsets in enumerate(INPUTS):
            for n, offset in enumerate(offsets):

                def forward(blocks, quarter, slots, role=role, n=n, offset=offset):
                    peer = z_peer(NZ - offset + RELAYS[role])
                    i = 3 * role + n
                    col = slots.start
                    remote(
                        zqs.at[blocks], rrs.at[role, n, slots], r_send.at[1, i], r_recv.at[1, role, col], peer
                    ).start()
                    remote(
                        zq.at[blocks, quarter], rr.at[role, n, slots], r_send.at[0, i], r_recv.at[0, role, col], peer
                    ).start()

                for_owner(piece, offset, forward)

    def for_owner(piece, offset, action):
        stage, blocks = PIECES[piece]
        owner = lax.rem(z + NZ - offset, NZ)
        pair = lax.div(lax.rem(owner, 8), 2)
        quarter = 2 * lax.div(owner, 8) + lax.rem(owner, 2)
        if blocks[0][0] == stage:

            @pl.when(pair == stage)
            def _():
                action(pl.ds(FIRST[piece], len(blocks)), quarter, pl.ds(blocks[0][1], len(blocks)))

        else:

            @pl.when(pair < stage)
            def _():
                action(pl.ds(FIRST[piece] + pair, 1), quarter, pl.ds(stage, 1))

    def z_relay(piece):
        for role, offset in enumerate(RELAYS):

            def pass_on(blocks, quarter, slots, role=role, offset=offset):
                inputs, col = len(INPUTS[role]), slots.start
                wait_for(rrs.at[role, pl.ds(0, inputs), slots], r_recv.at[1, role, col])
                wait_for(rr.at[role, pl.ds(0, inputs), slots], r_recv.at[0, role, col])
                rows = pl.ds(pl.multiple_of(quarter * 16, 16), 16)
                for i in range(slots.size):
                    total = own[blocks.start + i, rows, :]
                    for n in range(inputs):
                        total = total + from_fixed(rr[role, n, col + i], rrs[role, n, col + i])
                    rq[role, col + i], rqs[role, col + i] = to_fixed(total)
                peer = z_peer(NZ - offset)
                remote(rqs.at[role, slots], zrs.at[role, slots], z_send.at[1, role], z_recv.at[1, col], peer).start()
                remote(rq.at[role, slots], zr.at[role, slots], z_send.at[0, role], z_recv.at[0, col], peer).start()

            for_owner(piece, offset, pass_on)

    def of_stage(stage, step):
        for piece, (its_stage, _) in enumerate(PIECES):
            if its_stage == stage:
                step(piece)

    def spread(n, landing, peer):
        for d in range(1, landing.shape[0] + 1):
            remote(en.at[n], landing.at[d - 1], e_send.at[n], e_recv.at[n], peer(d)).start()

    def gather(n, landing):
        wait_for(landing, e_recv.at[n])
        return en[n] + jnp.sum(landing[...], axis=0)

    energy = jnp.zeros((1, 2 * QB), F32)
    for pair in range(PAIRS):
        energy = lax.fori_loop(0, TOK // QB, functools.partial(attend, pair), energy, unroll=4)
        if pair == PAIRS - 1:
            en[0] = energy[:, 0:QB] + energy[:, QB:]
            spread(0, enz, z_peer)
        of_stage(pair - 3, z_relay)
        of_stage(pair - 2, z_stage)
        of_stage(pair, y_stage)
    last = [piece for piece, (stage, _) in enumerate(PIECES) if stage == PAIRS - 1]
    of_stage(PAIRS - 3, z_relay)
    of_stage(PAIRS - 2, z_stage)
    en[1] = gather(0, enz)
    spread(1, ent, t_peer)
    of_stage(PAIRS - 2, z_relay)
    z_stage(last[0])
    en[2] = gather(1, ent)
    spread(2, eny, y_peer)
    z_stage(last[1])
    z_relay(last[0])
    z_relay(last[1])

    my_pair = lax.div(lax.rem(z, 8), 2)
    my_quarter = 2 * lax.div(z, 8) + lax.rem(z, 2)
    all_energy = jnp.sum(gather(2, eny), axis=1, keepdims=True)
    gain = (HEADS * HD) / all_energy
    for piece in range(len(PIECES)):

        def arrive(blocks, quarter, slots):
            wait_for(zrs.at[:, slots], z_recv.at[1, slots.start])
            wait_for(zr.at[:, slots], z_recv.at[0, slots.start])

        for_owner(piece, 0, arrive)

    row_id = dp * 16 + lax.broadcasted_iota(jnp.int32, (16, HD), 0)
    col_id = lax.broadcasted_iota(jnp.int32, (16, HD), 1)
    my_rows = pl.ds(pl.multiple_of(my_quarter * 16, 16), 16)
    for col in range(PAIRS):
        k = sum(jnp.where(my_pair == row, NUMBER[row, col], 0) for row in range(PAIRS))
        total = own[k, my_rows, :]
        for role in range(len(RELAYS)):
            total = total + from_fixed(zr[role, col], zrs[role, col])
        for half in range(2):
            head = col + PAIRS * half
            part = total[:, half * HD : (half + 1) * HD] * gain
            eye = jnp.where(row_id == col_id + head * HD, damping, 0.0)
            out_ref[:, head * HD : (head + 1) * HD] = part + eye

    for copy in halo:
        copy.wait_send()
    for piece, (_, blocks) in enumerate(PIECES):
        span = pl.ds(FIRST[piece], len(blocks))
        wait_for(yrs.at[:, span], y_send.at[1, piece])
        wait_for(yr.at[:, span], y_send.at[0, piece])
    for role, offsets in enumerate(INPUTS):
        for n in range(len(offsets)):
            wait_for(rrs.at[role, n], r_send.at[1, 3 * role + n])
            wait_for(rr.at[role, n], r_send.at[0, 3 * role + n])
        wait_for(zrs.at[role], z_send.at[1, role])
        wait_for(zr.at[role], z_send.at[0, role])
    for n, landing in enumerate((enz, ent, eny)):
        wait_for(landing, e_send.at[n])


def on_device(queries, key_heads, value_heads, doc_lengths):
    blocks = PAIRS * PAIRS
    width = 2 * HD
    roles = len(RELAYS)
    vmem = pl.BlockSpec(memory_space=pltpu.VMEM)
    rows = pl.pallas_call(
        kernel,
        out_shape=jax.ShapeDtypeStruct((16, 8 * HD), F32),
        in_specs=[pl.BlockSpec(memory_space=pl.ANY)] * 4,
        out_specs=vmem,
        scratch_shapes=[
            pltpu.VMEM((1, doc_lengths.shape[0]), jnp.int32),
            pltpu.VMEM((TOK, 8 * HD), jnp.bfloat16),
            pltpu.VMEM((2 * TOK, HD), jnp.bfloat16),
            pltpu.VMEM((2 * TOK, HD), jnp.bfloat16),
            pltpu.VMEM((HD, 2 * TOK), jnp.bfloat16),
            pltpu.VMEM((TOK // QB, WIN, QB), F32),
            pltpu.VMEM((PAIRS, width, TOK), jnp.bfloat16),
            pltpu.VMEM((width, width), F32),
            pltpu.VMEM((blocks, 64, width), F32),
            pltpu.VMEM((NY, blocks, 64, width), jnp.int16),
            pltpu.VMEM((blocks, 1, width), F32),
            pltpu.VMEM((NY - 1, blocks, 64, width), jnp.int16),
            pltpu.VMEM((NY - 1, blocks, 1, width), F32),
            pltpu.VMEM((blocks, 4, 16, width), jnp.int16),
            pltpu.VMEM((blocks, 1, width), F32),
            pltpu.VMEM((roles, 3, PAIRS, 16, width), jnp.int16),
            pltpu.VMEM((roles, 3, PAIRS, 1, width), F32),
            pltpu.VMEM((roles, PAIRS, 16, width), jnp.int16),
            pltpu.VMEM((roles, PAIRS, 1, width), F32),
            pltpu.VMEM((roles, PAIRS, 16, width), jnp.int16),
            pltpu.VMEM((roles, PAIRS, 1, width), F32),
            pltpu.VMEM((3, 1, HD), F32),
            pltpu.VMEM((NT - 1, 1, HD), F32),
            pltpu.VMEM((NY - 1, 1, HD), F32),
            pltpu.VMEM((NZ - 1, 1, HD), F32),
            pltpu.SemaphoreType.DMA((4,)),
            pltpu.SemaphoreType.DMA((2,)),
            pltpu.SemaphoreType.DMA((2,)),
            pltpu.SemaphoreType.DMA((2, len(PIECES))),
            pltpu.SemaphoreType.DMA((2, len(PIECES))),
            pltpu.SemaphoreType.DMA((2, 3 * roles)),
            pltpu.SemaphoreType.DMA((2, roles, PAIRS)),
            pltpu.SemaphoreType.DMA((2, roles)),
            pltpu.SemaphoreType.DMA((2, PAIRS)),
            pltpu.SemaphoreType.DMA((3,)),
            pltpu.SemaphoreType.DMA((3,)),
        ],
        compiler_params=pltpu.CompilerParams(
            collective_id=0, has_side_effects=True, vmem_limit_bytes=60 << 20
        ),
        name="attend_and_gram",
    )(doc_lengths.reshape(1, -1), queries, key_heads, value_heads)
    return rows[None]


def solution(mesh):
    placed = (P("dp", "tensor"), P("dp", "tensor"), P("dp", "tensor"), P())
    return jax.shard_map(
        on_device, mesh=mesh, in_specs=placed, out_specs=P("tensor", "dp", None), check_vma=False
    )
```

time: 76.1 us -> 65 us (0.85)
  the two profiles are of different devices: /device:TPU:32 before, /device:TPU:24 now
where the time goes in v2:
time: 65 us; the launch traced here: 64.1 us
  Pallas kernels  62.6 us (96%)
  local copies, waits for them, and re-layouts  1.47 us (2%)
    pallas_call x1, Pallas kernels, on_device(): pl.pallas_call(kernel, out_shape=jax.ShapeDtypeStruct((16, 8 * HD), F32),...  62.6 us
    unnamed x1, local copies, waits for them, and re-layouts  1.47 us

profile of v2, /device:TPU:24, one launch (start us, length us, event | category | flops | bytes accessed | tf_op | source)
XLA Modules:
  0.0 64.1 jit_solution(1334730792612431503)
XLA Ops:
  0.0 62.6 %attend_and_gram.1 = f32[16,1024]{1,0:T(8,128)} custom-call(s32[1,256]{1,0:T(1,128)} %bitcast.3, bf16[512,1024]{1,0:T(8,128)(2,1)} %q_hbm.1, bf16[512,128]{1,0:T(8,128)(2,1)} %k_hbm.1, bf16[512,128]{1,0:T(8,128)(2,1)} %v_hbm.1), custom_call_target="tpu_custom_call" | custom-call | tf_op jit(solution)/shard_map/attend_and_gram/pallas_call | solution.py:323
  62.6 1.5 %copy.6 = f32[1,16,1024]{2,1,0:T(8,128)} copy(f32[1,16,1024]{2,1,0:T(8,128)} %bitcast.2) | data formatting | bytes 131072

commit v3 on v2

--- a/solution.py
+++ b/solution.py
@@ -97,10 +97,13 @@
         load.start()
 
     pl.semaphore_wait(barrier, len(peers))
-    halo = [
-        remote(k_hbm, keys.at[earlier], h_send.at[0], h_recv.at[0], following),
-        remote(v_hbm, vals.at[earlier], h_send.at[1], h_recv.at[1], following),
-    ]
+    halo = []
+    for b in reversed(range(TOK // QB)):
+        rows = pl.ds(b * QB, QB)
+        halo += [
+            remote(src.at[rows], dst.at[rows], h_send.at[i, b], h_recv.at[i, b], following)
+            for i, (src, dst) in enumerate(((k_hbm, keys), (v_hbm, vals)))
+        ]
     for copy in halo:
         copy.start()
 
@@ -121,9 +124,6 @@
     for load in loads[1:]:
         load.wait()
     vt[:, TOK:] = vals[TOK:].T
-    for copy in halo:
-        copy.wait_recv()
-    vt[:, 0:TOK] = vals[0:TOK].T
 
     factor = math.log2(math.e) / math.sqrt(HD)
 
@@ -253,16 +253,25 @@
 
     energy = jnp.zeros((1, 2 * QB), F32)
     for pair in range(PAIRS):
-        energy = lax.fori_loop(0, TOK // QB, functools.partial(attend, pair), energy, unroll=4)
+        if pair == 0:
+            for n, b in enumerate(reversed(range(TOK // QB))):
+                for copy in halo[2 * n : 2 * n + 2]:
+                    copy.wait_recv()
+                rows = slice(b * QB, (b + 1) * QB)
+                vt[:, rows] = vals[rows].T
+                energy = attend(pair, jnp.int32(b), energy)
+        else:
+            energy = lax.fori_loop(0, TOK // QB, functools.partial(attend, pair), energy, unroll=4)
         if pair == PAIRS - 1:
             en[0] = energy[:, 0:QB] + energy[:, QB:]
             spread(0, enz, z_peer)
-        of_stage(pair - 3, z_relay)
-        of_stage(pair - 2, z_stage)
         of_stage(pair, y_stage)
     last = [piece for piece, (stage, _) in enumerate(PIECES) if stage == PAIRS - 1]
+    of_stage(0, z_stage)
+    of_stage(1, z_stage)
+    of_stage(0, z_relay)
+    of_stage(PAIRS - 2, z_stage)
     of_stage(PAIRS - 3, z_relay)
-    of_stage(PAIRS - 2, z_stage)
     en[1] = gather(0, enz)
     spread(1, ent, t_peer)
     of_stage(PAIRS - 2, z_relay)
@@ -352,8 +361,8 @@
             pltpu.VMEM((NY - 1, 1, HD), F32),
             pltpu.VMEM((NZ - 1, 1, HD), F32),
             pltpu.SemaphoreType.DMA((4,)),
-            pltpu.SemaphoreType.DMA((2,)),
-            pltpu.SemaphoreType.DMA((2,)),
+            pltpu.SemaphoreType.DMA((2, TOK // QB)),
+            pltpu.SemaphoreType.DMA((2, TOK // QB)),
             pltpu.SemaphoreType.DMA((2, len(PIECES))),
             pltpu.SemaphoreType.DMA((2, len(PIECES))),
             pltpu.SemaphoreType.DMA((2, 3 * roles)),

time: 65 us -> 63.6 us (0.978)
  Pallas kernels: 62.6 us -> 61 us
    pallas_call x1, Pallas kernels: 62.6 us -> 61 us  [on_device(): pl.pallas_call(kernel, out_shape=jax.ShapeDtypeStruct((16, 8 * HD), F32),...]
where the time goes in v3:
time: 63.6 us; the launch traced here: 62.5 us
  Pallas kernels  61 us (96%)
  local copies, waits for them, and re-layouts  1.47 us (2%)
    pallas_call x1, Pallas kernels, on_device(): pl.pallas_call(kernel, out_shape=jax.ShapeDtypeStruct((16, 8 * HD), F32),...  61 us
    unnamed x1, local copies, waits for them, and re-layouts  1.47 us

profile of v3, /device:TPU:24, one launch (start us, length us, event | category | flops | bytes accessed | tf_op | source)
XLA Modules:
  0.0 62.5 jit_solution(6079336682512523986)
XLA Ops:
  0.0 61.0 %attend_and_gram.1 = f32[16,1024]{1,0:T(8,128)} custom-call(s32[1,256]{1,0:T(1,128)} %bitcast.3, bf16[512,1024]{1,0:T(8,128)(2,1)} %q_hbm.1, bf16[512,128]{1,0:T(8,128)(2,1)} %k_hbm.1, bf16[512,128]{1,0:T(8,128)(2,1)} %v_hbm.1), custom_call_target="tpu_custom_call" | custom-call | tf_op jit(solution)/shard_map/attend_and_gram/pallas_call | solution.py:332
  61.0 1.5 %copy.6 = f32[1,16,1024]{2,1,0:T(8,128)} copy(f32[1,16,1024]{2,1,0:T(8,128)} %bitcast.2) | data formatting | bytes 131072

commit v4 on v3

--- a/solution.py
+++ b/solution.py
@@ -41,8 +41,6 @@
 
 PIECES = plan()
 FIRST = [sum(len(blocks) for _, blocks in PIECES[:n]) for n in range(len(PIECES))]
-NUMBER = {block: k for k, block in enumerate(block for _, blocks in PIECES for block in blocks)}
-
 
 def to_fixed(block):
     peak = jnp.maximum(jnp.max(jnp.abs(block), axis=0, keepdims=True), 1e-30)
@@ -159,7 +157,7 @@
             for a in range(NY):
                 low = q * 64 + a * 16
                 yq[a, k, q * 16 : (q + 1) * 16, :] = fixed[low : low + 16, :]
-            own[k, q * 16 : (q + 1) * 16, :] = gs[pl.ds(pl.multiple_of(q * 64 + y * 16, 16), 16), :]
+            own[PAIRS * row + col, q * 16 : (q + 1) * 16, :] = gs[pl.ds(pl.multiple_of(q * 64 + y * 16, 16), 16), :]
 
     def y_stage(piece):
         first, blocks = FIRST[piece], PIECES[piece][1]
@@ -172,20 +170,23 @@
             remote(yqs.at[span], yrs.at[d - 1, span], y_send.at[1, piece], y_recv.at[1, piece], peer).start()
             remote(yq.at[to, span], yr.at[d - 1, span], y_send.at[0, piece], y_recv.at[0, piece], peer).start()
 
-    def z_stage(piece):
-        first, blocks = FIRST[piece], PIECES[piece][1]
-        span = pl.ds(first, len(blocks))
-        wait_for(yrs.at[:, span], y_recv.at[1, piece])
-        wait_for(yr.at[:, span], y_recv.at[0, piece])
-        for k in range(first, first + len(blocks)):
-            total = own[k]
-            for d in range(NY - 1):
-                total = total + from_fixed(yr[d, k], yrs[d, k])
-            own[k] = total
-            fixed, scale = to_fixed(total)
-            zqs[k] = scale
-            for q in range(4):
-                zq[k, q] = fixed[q * 16 : (q + 1) * 16, :]
+    def z_stage(part):
+        for piece, (stage, blocks) in enumerate(PIECES):
+            if part != (0 if stage < PAIRS - 1 else 1 if blocks[0][0] == stage else 2):
+                continue
+            span = pl.ds(FIRST[piece], len(blocks))
+            wait_for(yrs.at[:, span], y_recv.at[1, piece])
+            wait_for(yr.at[:, span], y_recv.at[0, piece])
+            for i, (row, col) in enumerate(blocks):
+                k, place = FIRST[piece] + i, PAIRS * row + col
+                total = own[place]
+                for d in range(NY - 1):
+                    total = total + from_fixed(yr[d, k], yrs[d, k])
+                own[place] = total
+                fixed, scale = to_fixed(total)
+                zqs[place] = scale
+                for q in range(4):
+                    zq[place, q] = fixed[q * 16 : (q + 1) * 16, :]
         for role, offsets in enumerate(INPUTS):
             for n, offset in enumerate(offsets):
 
@@ -200,26 +201,19 @@
                         zq.at[blocks, quarter], rr.at[role, n, slots], r_send.at[0, i], r_recv.at[0, role, col], peer
                     ).start()
 
-                for_owner(piece, offset, forward)
-
-    def for_owner(piece, offset, action):
-        stage, blocks = PIECES[piece]
+                for_owner(part, offset, forward)
+
+    def for_owner(part, offset, action):
         owner = lax.rem(z + NZ - offset, NZ)
         pair = lax.div(lax.rem(owner, 8), 2)
         quarter = 2 * lax.div(owner, 8) + lax.rem(owner, 2)
-        if blocks[0][0] == stage:
-
-            @pl.when(pair == stage)
-            def _():
-                action(pl.ds(FIRST[piece], len(blocks)), quarter, pl.ds(blocks[0][1], len(blocks)))
-
-        else:
-
-            @pl.when(pair < stage)
-            def _():
-                action(pl.ds(FIRST[piece] + pair, 1), quarter, pl.ds(stage, 1))
-
-    def z_relay(piece):
+        low, count = ((0, PAIRS - 1), (0, PAIRS), (PAIRS - 1, 1))[part]
+
+        @pl.when(pair == PAIRS - 1 if part == 1 else pair < PAIRS - 1)
+        def _():
+            action(pl.ds(PAIRS * pair + low, count), quarter, pl.ds(low, count))
+
+    def z_relay(part):
         for role, offset in enumerate(RELAYS):
 
             def pass_on(blocks, quarter, slots, role=role, offset=offset):
@@ -236,7 +230,7 @@
                 remote(rqs.at[role, slots], zrs.at[role, slots], z_send.at[1, role], z_recv.at[1, col], peer).start()
                 remote(rq.at[role, slots], zr.at[role, slots], z_send.at[0, role], z_recv.at[0, col], peer).start()
 
-            for_owner(piece, offset, pass_on)
+            for_owner(part, offset, pass_on)
 
     def of_stage(stage, step):
         for piece, (its_stage, _) in enumerate(PIECES):
@@ -267,39 +261,34 @@
             spread(0, enz, z_peer)
         of_stage(pair, y_stage)
     last = [piece for piece, (stage, _) in enumerate(PIECES) if stage == PAIRS - 1]
-    of_stage(0, z_stage)
-    of_stage(1, z_stage)
-    of_stage(0, z_relay)
-    of_stage(PAIRS - 2, z_stage)
-    of_stage(PAIRS - 3, z_relay)
+    z_stage(0)
     en[1] = gather(0, enz)
     spread(1, ent, t_peer)
-    of_stage(PAIRS - 2, z_relay)
-    z_stage(last[0])
+    z_relay(0)
+    z_stage(1)
     en[2] = gather(1, ent)
     spread(2, eny, y_peer)
-    z_stage(last[1])
-    z_relay(last[0])
-    z_relay(last[1])
+    z_stage(2)
+    z_relay(1)
+    z_relay(2)
 
     my_pair = lax.div(lax.rem(z, 8), 2)
     my_quarter = 2 * lax.div(z, 8) + lax.rem(z, 2)
     all_energy = jnp.sum(gather(2, eny), axis=1, keepdims=True)
     gain = (HEADS * HD) / all_energy
-    for piece in range(len(PIECES)):
+    for part in range(3):
 
         def arrive(blocks, quarter, slots):
             wait_for(zrs.at[:, slots], z_recv.at[1, slots.start])
             wait_for(zr.at[:, slots], z_recv.at[0, slots.start])
 
-        for_owner(piece, 0, arrive)
+        for_owner(part, 0, arrive)
 
     row_id = dp * 16 + lax.broadcasted_iota(jnp.int32, (16, HD), 0)
     col_id = lax.broadcasted_iota(jnp.int32, (16, HD), 1)
     my_rows = pl.ds(pl.multiple_of(my_quarter * 16, 16), 16)
     for col in range(PAIRS):
-        k = sum(jnp.where(my_pair == row, NUMBER[row, col], 0) for row in range(PAIRS))
-        total = own[k, my_rows, :]
+        total = own[PAIRS * my_pair + col, my_rows, :]
         for role in range(len(RELAYS)):
             total = total + from_fixed(zr[role, col], zrs[role, col])
         for half in range(2):

time: 63.6 us -> 66.4 us (1.044); the launches traced: 62.5 us -> 66.2 us
  Pallas kernels: 61 us -> 64.7 us
    pallas_call x1, Pallas kernels: 61 us -> 64.7 us  [on_device(): pl.pallas_call(kernel, out_shape=jax.ShapeDtypeStruct((16, 8 * HD), F32),...]
where the time goes in v4:
time: 66.4 us; the launch traced here: 66.2 us
  Pallas kernels  64.7 us (97%)
  local copies, waits for them, and re-layouts  1.47 us (2%)
    pallas_call x1, Pallas kernels, on_device(): pl.pallas_call(kernel, out_shape=jax.ShapeDtypeStruct((16, 8 * HD), F32),...  64.7 us
    unnamed x1, local copies, waits for them, and re-layouts  1.47 us

profile of v4, /device:TPU:24, one launch (start us, length us, event | category | flops | bytes accessed | tf_op | source)
XLA Modules:
  0.0 66.2 jit_solution(12932727745215986596)
XLA Ops:
  0.0 64.7 %attend_and_gram.1 = f32[16,1024]{1,0:T(8,128)} custom-call(s32[1,256]{1,0:T(1,128)} %bitcast.3, bf16[512,1024]{1,0:T(8,128)(2,1)} %q_hbm.1, bf16[512,128]{1,0:T(8,128)(2,1)} %k_hbm.1, bf16[512,128]{1,0:T(8,128)(2,1)} %v_hbm.1), custom_call_target="tpu_custom_call" | custom-call | tf_op jit(solution)/shard_map/attend_and_gram/pallas_call | solution.py:321
  64.7 1.5 %copy.6 = f32[1,16,1024]{2,1,0:T(8,128)} copy(f32[1,16,1024]{2,1,0:T(8,128)} %bitcast.2) | data formatting | bytes 131072
